TPU v7x, 1024 devices: a whole 4x8x16 slice. The times are simulated.
1024 devices in a mesh: ctx: 64 (over y, z_hi, x), dp: 16 (over z_lo, core).
Axes of the slice: x: 4, y: 8, z: 16 (z_hi: 2, z_lo: 8; z = z_hi * 8 + z_lo), core: 2. Of those that a mesh axis runs over, the one named last changes fastest.
Arguments:
- query: bfloat16 [16, 8192, 512], P('dp', 'ctx'), may hold values from -20 to 20
- key: bfloat16 [16, 8192, 512], P('dp', 'ctx'), may hold values from -20 to 20
- value: bfloat16 [16, 8192, 512], P('dp', 'ctx'), may hold values from -6 to 6
- table: int32 [128, 4], P('ctx'), may hold values from 0 to 127, as said below
- out_weight: bfloat16 [512, 512], replicated, may hold values from -0.25 to 0.25
- cotangent: bfloat16 [16, 8192, 512], P('dp', 'ctx'), may hold values from -6 to 6
Outputs:
- layer_out: bfloat16 [16, 8192, 512], P('dp', 'ctx')
- grad_query: bfloat16 [16, 8192, 512], P('dp', 'ctx')
- grad_key: bfloat16 [16, 8192, 512], P('dp', 'ctx')
- grad_value: bfloat16 [16, 8192, 512], P('dp', 'ctx')
- grad_weight: float32 [512, 512], replicated
Inputs may be any that keep to these rules, and one draw needn't show every extreme that they name: `table`: row b names block b first; its other three ids are distinct, differ from b, and name blocks held on the same index of ctx as b or on the index just before or just after it, cyclically, where index c holds blocks c * 2 to (c + 1) * 2 - 1.
All inputs are finite; a program needn't handle non-finite values.
Results may differ from a plain program's by a relative error of at most 0.0086.
Values may be sent and summed in bfloat16 or wider, within the bound.
A program may use at most 32 MiB of HBM per device.

v0:
```python
import math

import jax
import jax.numpy as jnp
from jax import lax
from jax.sharding import PartitionSpec as P

H = 8
BS = 64


def with_halo(array, sides, width):
    for axis, dim in sides:
        size, length = (lax.axis_size(axis), array.shape[dim])
        up = [(i, (i + 1) % size) for i in range(size)]
        down = [(j, i) for i, j in up]
        last = lax.slice_in_dim(array, length - width, length, axis=dim)
        initial = lax.slice_in_dim(array, 0, width, axis=dim)
        before = lax.ppermute(last, axis, up)
        after = lax.ppermute(initial, axis, down)
        array = jnp.concatenate([before, array, after], axis=dim)
    return array


def passed_along(block, axis, distance):
    devices = range(lax.axis_size(axis))
    route = [((i - distance) % len(devices), i) for i in devices]
    return lax.ppermute(block, axis, route)


def local_pass(local_query, key_window, value_window, candidate, local_grad):
    block_count = candidate.shape[0]
    width = local_query.shape[1]
    head_size = width // H
    scale = 1.0 / math.sqrt(head_size)
    key_blocks = key_window.reshape(3 * block_count, BS, width)[candidate].reshape(
        block_count, 4 * BS, H, head_size
    )
    value_blocks = value_window.reshape(3 * block_count, BS, width)[candidate].reshape(
        block_count, 4 * BS, H, head_size
    )
    query_blocks = local_query.reshape(block_count, BS, H, head_size)
    grad_blocks = local_grad.reshape(block_count, BS, H, head_size)
    scores = (
        jnp.einsum("bqhe,bkhe->bhqk", query_blocks, key_blocks, preferred_element_type=jnp.float32)
        * scale
    )
    row_max = jnp.max(scores, axis=-1, keepdims=True)
    log_total = row_max + jnp.log(jnp.sum(jnp.exp(scores - row_max), axis=-1, keepdims=True))
    weights = jnp.exp(scores - log_total)
    rounded = weights.astype(jnp.bfloat16)
    attn = (
        jnp.einsum("bhqk,bkhe->bqhe", rounded, value_blocks, preferred_element_type=jnp.float32)
        .astype(jnp.bfloat16)
        .reshape(block_count * BS, width)
    )
    dprob = jnp.einsum(
        "bqhe,bkhe->bhqk", grad_blocks, value_blocks, preferred_element_type=jnp.float32
    )
    delta = jnp.sum(weights * dprob, axis=-1, keepdims=True)
    dscore = (weights * (dprob - delta) * scale).astype(jnp.bfloat16)
    grad_query = (
        jnp.einsum("bhqk,bkhe->bqhe", dscore, key_blocks, preferred_element_type=jnp.float32)
        .astype(jnp.bfloat16)
        .reshape(block_count * BS, width)
    )
    key_terms = jnp.einsum(
        "bhqk,bqhe->bkhe", dscore, query_blocks, preferred_element_type=jnp.float32
    ).reshape(block_count * 4, BS, width)
    value_terms = jnp.einsum(
        "bhqk,bqhe->bkhe", rounded, grad_blocks, preferred_element_type=jnp.float32
    ).reshape(block_count * 4, BS, width)
    selector = (
        candidate.reshape(-1)[:, None] == jnp.arange(3 * block_count, dtype=jnp.int32)[None, :]
    ).astype(jnp.float32)
    key_window_grad = jnp.einsum(
        "nc,nsf->csf", selector, key_terms, precision=lax.Precision.HIGHEST
    )
    value_window_grad = jnp.einsum(
        "nc,nsf->csf", selector, value_terms, precision=lax.Precision.HIGHEST
    )
    return (attn, grad_query, key_window_grad, value_window_grad)


def body(query, key, value, table, out_weight, cotangent):
    local_query = query[0]
    local_key = key[0]
    local_value = value[0]
    local_cotan = cotangent[0]
    block_count = table.shape[0]
    token_count = local_query.shape[0]
    width = local_query.shape[1]
    device_index = lax.axis_index("ctx")
    total_blocks = block_count * lax.axis_size("ctx")
    candidate = jnp.mod(table - (device_index - 1) * block_count, total_blocks)
    stacked = jnp.stack([local_key, local_value])
    window = with_halo(stacked, (("ctx", 1),), token_count)
    grad_attn = lax.dot_general(
        local_cotan, out_weight, (((1,), (1,)), ((), ())), preferred_element_type=jnp.float32
    ).astype(jnp.bfloat16)
    attn, grad_q, key_window_grad, value_window_grad = local_pass(
        local_query, window[0], window[1], candidate, grad_attn
    )
    layer_out = jnp.dot(attn, out_weight, preferred_element_type=jnp.float32).astype(jnp.bfloat16)
    weight_term = lax.dot_general(
        attn, local_cotan, (((0,), (0,)), ((), ())), preferred_element_type=jnp.float32
    )
    weight_total = lax.psum(weight_term, ("ctx", "dp"))
    grad_weight = weight_total / math.sqrt(lax.axis_size("dp") * lax.axis_size("ctx") * token_count)
    key_parts = key_window_grad.reshape(3, token_count, width).astype(jnp.bfloat16)
    value_parts = value_window_grad.reshape(3, token_count, width).astype(jnp.bfloat16)
    lower_parts = jnp.stack([key_parts[0], value_parts[0]])
    upper_parts = jnp.stack([key_parts[2], value_parts[2]])
    own_parts = jnp.stack([key_parts[1], value_parts[1]]).astype(jnp.float32)
    from_after = passed_along(lower_parts, "ctx", -1)
    from_before = passed_along(upper_parts, "ctx", 1)
    summed = (own_parts + from_after.astype(jnp.float32) + from_before.astype(jnp.float32)).astype(
        jnp.bfloat16
    )
    return (layer_out[None], grad_q[None], summed[0][None], summed[1][None], grad_weight)


def solution(mesh):
    return jax.shard_map(
        body,
        mesh=mesh,
        in_specs=(
            P("dp", "ctx", None),
            P("dp", "ctx", None),
            P("dp", "ctx", None),
            P("ctx", None),
            P(),
            P("dp", "ctx", None),
        ),
        out_specs=(
            P("dp", "ctx", None),
            P("dp", "ctx", None),
            P("dp", "ctx", None),
            P("dp", "ctx", None),
            P(),
        ),
        check_vma=False,
    )
```

profile of v0, /device:TPU:1, one launch (start us, length us, event | category | flops | bytes accessed | tf_op | source)
XLA Modules:
  0.0 604.2 jit_solution(1597116654395975174)
XLA Ops:
  7.2 1.0 constant_dynamic-update-slice_fusion.1
  8.2 0.9 constant_dynamic-update-slice_fusion
  9.1 25.0 %collective-permute-start.1 = (bf16[2,128,512]{2,1,0:T(8,128)(2,1)S(1)}, bf16[2,128,512]{2,1,0:T(8,128)(2,1)S(1)}, u32[]{:S(2)}, u32[]{:S(2)}) collective-permute-start(bf16[2,128,512]{2,1,0:T(8,128)(2,1)S(1)} %constant_dynamic-update-slice_fusion), channel_id=1, source_target_pairs={{16,0},{32,16},{48,32},{64,48},{80,64},{96,80},{112,96},{128,112},... | collective-permute-start | bytes 786440 | tf_op jit(solution)/shard_map/ppermute | solution.py:20
  34.1 1.9 collective-permute-start
  36.1 0.7 compare_select_fusion
  36.9 1.2 convolution_convert_fusion.4
  38.8 0.9 copy.23
  39.7 15.3 %collective-permute-done.1 = bf16[2,128,512]{2,1,0:T(8,128)(2,1)S(1)} collective-permute-done((bf16[2,128,512]{2,1,0:T(8,128)(2,1)S(1)}, bf16[2,128,512]{2,1,0:T(8,128)(2,1)S(1)}, u32[]{:S(2)}, u32[]{:S(2)}) %collective-permute-start.1) | collective-permute-done | bytes 262176 | tf_op jit(solution)/shard_map/ppermute | solution.py:20
  55.0 16.2 %collective-permute-done = bf16[2,128,512]{2,1,0:T(8,128)(2,1)S(1)} collective-permute-done((bf16[2,128,512]{2,1,0:T(8,128)(2,1)S(1)}, bf16[2,128,512]{2,1,0:T(8,128)(2,1)S(1)}, u32[]{:S(2)}, u32[]{:S(2)}) %collective-permute-start) | collective-permute-done | bytes 262176 | tf_op jit(solution)/shard_map/ppermute | solution.py:19
  75.7 1.3 fusion.42
  77.0 1.1 fusion.6
  78.5 8.1 %convolution_bitcast_fusion = f32[2,256,8,64]{1,3,2,0:T(8,128)} fusion(bf16[2,64,8,64]{1,3,2,0:T(8,128)(2,1)} %copy.23, f32[2,8,64,256]{3,2,1,0:T(8,128)} %fusion.42, f32[2,8,64,256]{3,2,1,0:T(8,128)S(1)} %get-tuple-element.18, f32[2,8,64]{2,1,0:T(8,128)S(1)} %log_add_fusion), kind=kOutput, calls=%fused_computation.6 | convolution fusion | flops 35390720 | bytes 3280896 | tf_op jit(solution)/shard_map/bhqk,bqhe->bkhe/dot_general | solution.py:67
  86.6 0.9 copy.18
  87.5 1.2 reshape.51
  88.7 1.3 fusion.24
  90.0 2.0 copy.28
  91.9 1.9 reshape.54
  93.9 1.2 convolution_convert_fusion
  95.4 0.7 copy.32
  96.3 2.0 copy.24
  98.3 1.9 reshape.53
  100.2 1.2 convolution_convert_fusion.1
  101.8 1.9 collective-permute-start.2
  103.7 3.4 collective-permute-start.3
  107.1 7.1 %fusion.7 = bf16[2,64,8,64]{1,3,2,0:T(8,128)(2,1)S(1)} fusion(bf16[2,256,8,64]{1,3,2,0:T(8,128)(2,1)S(1)} %copy.15, f32[2,8,64,256]{3,2,1,0:T(8,128)} %fusion.42, f32[2,8,64,256]{3,2,1,0:T(8,128)S(1)} %get-tuple-element.18, f32[2,8,64]{2,1,0:T(8,128)S(1)} %log_add_fusion), kind=kOutput, calls=%fused_computation.16 | convolution fusion | flops 35456256 | bytes 2756608 | tf_op jit(solution)/shard_map/bhqk,bkhe->bqhe/dot_general | solution.py:63
  114.2 0.9 fusion.8
  115.3 0.9 broadcast_in_dim_reshape.4
  116.2 11.6 %collective-permute-done.3 = bf16[2,128,512]{2,1,0:T(8,128)(2,1)} collective-permute-done((bf16[2,128,512]{2,1,0:T(8,128)(2,1)S(1)}, bf16[2,128,512]{2,1,0:T(8,128)(2,1)}, u32[]{:S(2)}, u32[]{:S(2)}) %collective-permute-start.3) | collective-permute-done | bytes 262176 | tf_op jit(solution)/shard_map/ppermute | solution.py:28
  127.8 1.1 add_convert_fusion
  129.0 0.7 fusion.40
  129.7 465.3 %all-reduce.2.cloned.1.call-done = f32[512,512]{1,0:T(8,128)} async-done(((f32[512,512]{1,0:T(8,128)}), f32[512,512]{1,0:T(8,128)}) %all-reduce.2.cloned.1.call-update) | async-done | bytes 1048592 | tf_op jit(solution)/shard_map/psum | solution.py:108
  595.0 2.3 broadcast_multiply_fusion
  (45 shorter events, 6.7 us)
Async XLA Ops:
  7.2 29.8 %copy-start = (bf16[512,512]{1,0:T(8,128)(2,1)S(1)}, bf16[512,512]{1,0:T(8,128)(2,1)}, u32[]{:S(2)}) copy-start(bf16[512,512]{1,0:T(8,128)(2,1)} %param.10) | copy-start | bytes 1572868
  7.2 31.4 %copy-start.6 = (bf16[1,128,512]{2,1,0:T(8,128)(2,1)S(1)}, bf16[1,128,512]{2,1,0:T(8,128)(2,1)}, u32[]{:S(2)}) copy-start(bf16[1,128,512]{2,1,0:T(8,128)(2,1)} %param.6) | copy-start | bytes 393220
  7.2 587.8 %all-reduce.2.cloned.1.call-start = ((), (), s32[]{:S(2)}) async-start(), calls=%async_computation | async-start | bytes 2097152 | tf_op jit(solution)/shard_map/psum | solution.py:108
  9.1 45.9 %collective-permute-start.1 = (bf16[2,128,512]{2,1,0:T(8,128)(2,1)S(1)}, bf16[2,128,512]{2,1,0:T(8,128)(2,1)S(1)}, u32[]{:S(2)}, u32[]{:S(2)}) collective-permute-start(bf16[2,128,512]{2,1,0:T(8,128)(2,1)S(1)} %constant_dynamic-update-slice_fusion), channel_id=1, source_target_pairs={{16,0},{32,16},{48,32},{64,48},{80,64},{96,80},{112,96},{128,112},... | collective-permute-start | bytes 786440 | tf_op jit(solution)/shard_map/ppermute | solution.py:20
  34.1 37.1 %collective-permute-start = (bf16[2,128,512]{2,1,0:T(8,128)(2,1)S(1)}, bf16[2,128,512]{2,1,0:T(8,128)(2,1)S(1)}, u32[]{:S(2)}, u32[]{:S(2)}) collective-permute-start(bf16[2,128,512]{2,1,0:T(8,128)(2,1)S(1)} %constant_dynamic-update-slice_fusion), channel_id=1, source_target_pairs={{0,16},{16,32},{32,48},{48,64},{64,80},{80,96},{96,112},{112,128},... | collective-permute-start | bytes 786440 | tf_op jit(solution)/shard_map/ppermute | solution.py:19
  73.7 1.2 copy-start.2
  78.5 8.1 %copy-start.3 = (bf16[2,64,8,64]{1,3,2,0:T(8,128)(2,1)S(1)}, bf16[2,64,8,64]{1,3,2,0:T(8,128)(2,1)}, u32[]{:S(2)}) copy-start(bf16[2,64,8,64]{1,3,2,0:T(8,128)(2,1)} %fusion.6) | copy-start | bytes 393220
  78.5 10.2 %copy-start.4 = (bf16[1,128,512]{2,1,0:T(8,128)(2,1)S(1)}, bf16[1,128,512]{2,1,0:T(8,128)(2,1)}, u32[]{:S(2)}) copy-start(bf16[1,128,512]{2,1,0:T(8,128)(2,1)} %param.11) | copy-start | bytes 393220
  95.0 1.2 copy-start.1
  100.2 1.5 copy-start.5
  101.8 14.5 %collective-permute-start.2 = (bf16[2,128,512]{2,1,0:T(8,128)(2,1)S(1)}, bf16[2,128,512]{2,1,0:T(8,128)(2,1)}, u32[]{:S(2)}, u32[]{:S(2)}) collective-permute-start(bf16[2,128,512]{2,1,0:T(8,128)(2,1)S(1)} %pad_maximum_fusion.1), channel_id=1, source_target_pairs={{16,0},{32,16},{48,32},{64,48},{80,64},{96,80},{112,96},{128,112},... | collective-permute-start | bytes 786440 | tf_op jit(solution)/shard_map/ppermute | solution.py:28
  103.7 24.1 %collective-permute-start.3 = (bf16[2,128,512]{2,1,0:T(8,128)(2,1)S(1)}, bf16[2,128,512]{2,1,0:T(8,128)(2,1)}, u32[]{:S(2)}, u32[]{:S(2)}) collective-permute-start(bf16[2,128,512]{2,1,0:T(8,128)(2,1)S(1)} %pad_maximum_fusion.2), channel_id=1, source_target_pairs={{1008,0},{0,16},{16,32},{32,48},{48,64},{64,80},{80,96},{96,112},{... | collective-permute-start | bytes 786440 | tf_op jit(solution)/shard_map/ppermute | solution.py:28
Sparse Core Ops, SparseCore 0:
  114.3 480.6 all-reduce.1
where the time goes:
time: 605 us; the launch traced here: 604 us
  waiting for transfers between devices  509 us (84%)
  starting transfers between devices  32.3 us (5%)
  matrix products  24.1 us (4%)
  local copies, waits for them, and re-layouts  20.2 us (3%)
  between operations  14.4 us (2%)
    psum x1, waiting for transfers between devices, body(): weight_total = lax.psum(weight_term, ('ctx', 'dp'))  465 us
    ppermute x1, starting transfers between devices, with_halo(): after = lax.ppermute(initial, axis, down)  25 us
    ppermute x1, waiting for transfers between devices, with_halo(): before = lax.ppermute(last, axis, up)  16.2 us
    ppermute x1, waiting for transfers between devices, with_halo(): after = lax.ppermute(initial, axis, down)  15.3 us
  transfers between devices with their start and end apart: 5, of which 4 were waited for; matrix products, arithmetic and copies ran while one was open for 2% of the time, Pallas kernels for 0%

commit v1 on v0

v1 whole, which is shorter than its diff:
```python
import functools
import math

import jax
import jax.numpy as jnp
from jax import lax
from jax.experimental import pallas as pl
from jax.experimental.pallas import tpu as pltpu
from jax.sharding import PartitionSpec as P

MESH = pl.DeviceIdType.MESH
F32 = jnp.float32
BF16 = jnp.bfloat16

NX, NY, NZ, NC = 4, 8, 16, 2
ZLO = 8
TOK = 128
D = 512
BS = 64
PAIRS = 4
WIN = 3 * TOK


def place():
    ctx, dp = lax.axis_index("ctx"), lax.axis_index("dp")
    x = lax.rem(ctx, NX)
    zh = lax.rem(ctx // NX, NZ // ZLO)
    y = ctx // (NX * (NZ // ZLO))
    return ctx, dp, x, y, zh * ZLO + dp // NC, lax.rem(dp, NC)


def at(x, y, z, c):
    return (y * (NX * (NZ // ZLO)) + (z // ZLO) * NX + x, lax.rem(z, ZLO) * NC + c)


def nt(a, b):
    return lax.dot_general(a, b, (((1,), (1,)), ((), ())), preferred_element_type=F32)


def nn(a, b):
    return lax.dot_general(a, b, (((1,), (0,)), ((), ())), preferred_element_type=F32)


def tn(a, b):
    return lax.dot_general(a, b, (((0,), (0,)), ((), ())), preferred_element_type=F32)


def kernel(
    table, q, k, v, w, cot,
    layer_out, grad_q, grad_k, grad_v, grad_w,
    kwin, vwin, g, attn, bias,
    part_out, part_in, own,
    c_out, c_in, c_own, x_out, x_in, x_own, y_out, y_in, y_own, zall, gw,
    kv_s, kv_r, part_s, part_r, c_s, c_r, x_s, x_r, y_s, y_r, z_s, z_r,
    gy_s, gy_r, gx_s, gx_r, gc_s, gc_r,
):
    ctx, dp, x, y, z, c = place()
    n_ctx = lax.axis_size("ctx")
    before = (lax.rem(ctx + n_ctx - 1, n_ctx), dp)
    after = (lax.rem(ctx + 1, n_ctx), dp)
    other = at(x, y, z, 1 - c)
    xs = [lax.rem(x + i, NX) for i in range(NX)]
    ys = [lax.rem(y + i, NY) for i in range(NY)]
    zs = [lax.rem(z + i, NZ) for i in range(NZ)]

    barrier = pltpu.get_barrier_semaphore()
    peers = [before, after, other]
    peers += [at(i, y, z, c) for i in xs[1:]]
    peers += [at(x, i, z, c) for i in ys[1:]]
    peers += [at(x, y, i, c) for i in zs[1:]]
    for peer in peers:
        pl.semaphore_signal(barrier, 1, device_id=peer, device_id_type=MESH)
    pl.semaphore_wait(barrier, len(peers))

    def remote(src, dst, ssem, rsem, to):
        return pltpu.make_async_remote_copy(
            src_ref=src, dst_ref=dst, send_sem=ssem, recv_sem=rsem, device_id=to, device_id_type=MESH
        )

    def lanes(p):
        return pl.ds(p * 128, 128)

    halo = []
    for p in range(PAIRS):
        row = []
        for i, (src, win) in enumerate(((k, kwin), (v, vwin))):
            for j, (to, start) in enumerate(((after, 0), (before, 2 * TOK))):
                row.append(remote(
                    src.at[0, :, lanes(p)], win.at[pl.ds(start, TOK), lanes(p)],
                    kv_s.at[p, i, j], kv_r.at[p, i, j], to,
                ))
        for copy in row:
            copy.start()
        halo.append(row)

    kwin[pl.ds(TOK, TOK), :] = k[0]
    vwin[pl.ds(TOK, TOK), :] = v[0]
    g[...] = nt(cot[0], w[...]).astype(BF16)

    block = lax.broadcasted_iota(jnp.int32, (BS, WIN), 1) // BS
    for b in range(2):
        hit = None
        for j in range(4):
            cand = lax.rem(table[b, j] - (ctx - 1) * 2 + 2 * n_ctx, 2 * n_ctx)
            same = block == cand
            hit = same if hit is None else jnp.logical_or(hit, same)
        rows = jnp.where(hit, 0.0, -1e30).astype(F32)
        bias[pl.ds(b * BS, BS), :] = rows
        bias[pl.ds(TOK + b * BS, BS), :] = rows

    left = lax.broadcasted_iota(jnp.int32, (TOK, 128), 1) < 64

    def split(a):
        zero = jnp.zeros_like(a)
        return jnp.concatenate([jnp.where(left, a, zero), jnp.where(left, zero, a)], axis=0)

    def merged(a):
        return jnp.where(left, a[:TOK], a[TOK:])

    pending = []

    def send(copy):
        copy.start()
        pending.append(copy)

    def attention(p):
        for copy in halo[p]:
            copy.wait_recv()
        l = lanes(p)
        kw, vw = kwin[:, l], vwin[:, l]
        q2 = split(q[0, :, l] * jnp.asarray(0.125, BF16))
        s = nt(q2, kw) + bias[...]
        e = jnp.exp(s - jnp.max(s, axis=1, keepdims=True))
        weights = e * (1.0 / jnp.sum(e, axis=1, keepdims=True))
        rounded = weights.astype(BF16)
        out = merged(nn(rounded, vw)).astype(BF16)
        attn[:, l] = out
        term = tn(out, cot[0])
        c_own[p] = jnp.where(c == 0, term[:, :256], term[:, 256:])
        c_out[p] = jnp.where(c == 0, term[:, 256:], term[:, :256]).astype(BF16)
        send(remote(c_out.at[p], c_in.at[p], c_s.at[p], c_r.at[p], other))

        g2 = split(g[:, l])
        dprob = nt(g2, vw)
        delta = jnp.sum(weights * dprob, axis=1, keepdims=True)
        ds = (weights * (dprob - delta)).astype(BF16)
        dk = tn(ds, q2)
        dv = tn(rounded, g2)
        for i, d in enumerate((dk, dv)):
            part_out[i, 0, :, l] = d[:TOK].astype(BF16)
            part_out[i, 1, :, l] = d[2 * TOK:].astype(BF16)
            own[i, :, l] = d[TOK:2 * TOK]
            for j, to in enumerate((before, after)):
                send(remote(
                    part_out.at[i, j, :, l], part_in.at[i, j, :, l],
                    part_s.at[p, i, j], part_r.at[p, i, j], to,
                ))
        grad_q[0, :, l] = (merged(nn(ds, kw)) * 0.125).astype(BF16)

    def core_step(p):
        remote(c_out.at[p], c_in.at[p], c_s.at[p], c_r.at[p], other).wait_recv()
        total = c_own[p] + c_in[p].astype(F32)
        x_own[p] = total
        x_out[p] = total.astype(BF16)
        for i in range(1, NX):
            send(remote(
                x_out.at[p, pl.ds(xs[i] * 32, 32)], x_in.at[p, i - 1],
                x_s.at[p, i - 1], x_r.at[p, i - 1], at(xs[i], y, z, c),
            ))

    def x_step(p):
        total = x_own[p, pl.ds(x * 32, 32)]
        for i in range(1, NX):
            remote(
                x_out.at[p, pl.ds(xs[i] * 32, 32)], x_in.at[p, i - 1],
                x_s.at[p, i - 1], x_r.at[p, i - 1], at(xs[i], y, z, c),
            ).wait_recv()
            total = total + x_in[p, i - 1].astype(F32)
        y_out[p] = total.astype(BF16)
        for half in range(2):
            owner = 2 * p + half

            @pl.when(y == owner)
            def _():
                y_own[...] = total[half * 16:half * 16 + 16]

            @pl.when(y != owner)
            def _():
                slot = lax.rem(owner - y + NY, NY) - 1
                remote(
                    y_out.at[p, pl.ds(half * 16, 16)], y_in.at[slot],
                    y_s.at[p, half], y_r.at[slot], at(x, owner, z, c),
                ).start()

    def y_step():
        total = y_own[...]
        for i in range(NY - 1):
            remote(y_out.at[0, pl.ds(0, 16)], y_in.at[i], y_s.at[0, 0], y_r.at[i], other).wait_recv()
            total = total + y_in[i].astype(F32)
        zall[z] = total.astype(BF16)
        for i in range(1, NZ):
            send(remote(zall.at[z], zall.at[z], z_s.at[i - 1], z_r.at[z], at(x, y, zs[i], c)))

    def z_step():
        for i in range(1, NZ):
            remote(zall.at[z], zall.at[zs[i]], z_s.at[0], z_r.at[zs[i]], other).wait_recv()
        total = zall[0].astype(F32)
        for i in range(1, NZ):
            total = total + zall[i].astype(F32)
        gw[c, x, y] = total.astype(BF16)
        for i in range(1, NY):
            send(remote(gw.at[c, x, y], gw.at[c, x, y], gy_s.at[i - 1], gy_r.at[y], at(x, ys[i], z, c)))

    def gather_x():
        for i in range(1, NY):
            remote(gw.at[c, x, y], gw.at[c, x, ys[i]], gy_s.at[0], gy_r.at[ys[i]], other).wait_recv()
        for i in range(1, NX):
            send(remote(gw.at[c, x], gw.at[c, x], gx_s.at[i - 1], gx_r.at[x], at(xs[i], y, z, c)))

    def gather_core():
        for i in range(1, NX):
            remote(gw.at[c, x], gw.at[c, xs[i]], gx_s.at[0], gx_r.at[xs[i]], other).wait_recv()
        send(remote(gw.at[c], gw.at[c], gc_s, gc_r, other))

    attention(0)
    attention(1)
    core_step(0)
    attention(2)
    core_step(1)
    x_step(0)
    attention(3)
    core_step(2)
    x_step(1)
    core_step(3)
    x_step(2)
    x_step(3)
    y_step()
    layer_out[0] = nn(attn[...], w[...]).astype(BF16)
    z_step()
    gather_x()
    gather_core()

    for p in range(PAIRS):
        for i in range(2):
            for j, to in enumerate((before, after)):
                remote(
                    part_out.at[i, j, :, lanes(p)], part_in.at[i, j, :, lanes(p)],
                    part_s.at[p, i, j], part_r.at[p, i, j], to,
                ).wait_recv()
    for i, out in enumerate((grad_k, grad_v)):
        out[0] = (own[i] + part_in[i, 0].astype(F32) + part_in[i, 1].astype(F32)).astype(BF16)

    remote(gw.at[c], gw.at[1 - c], gc_s, gc_r, other).wait_recv()
    scale = 1.0 / math.sqrt(TOK * NX * NY * NZ * NC)
    for ci in range(NC):
        for yi in range(NY):
            for xi in range(NX):
                row = (yi // 2) * 128 + xi * 32 + (yi % 2) * 16
                grad_w[row:row + 16, ci * 256:ci * 256 + 256] = gw[ci, xi, yi].astype(F32) * scale

    for row in halo:
        for copy in row:
            copy.wait_send()
    for copy in pending:
        copy.wait_send()
    for p in range(PAIRS):
        for half in range(2):
            @pl.when(y != 2 * p + half)
            def _():
                remote(
                    y_out.at[p, pl.ds(half * 16, 16)], y_in.at[0],
                    y_s.at[p, half], y_r.at[0], other,
                ).wait_send()


def body(query, key, value, table, out_weight, cotangent):
    vmem = pl.BlockSpec(memory_space=pltpu.VMEM)
    dma = pltpu.SemaphoreType.DMA
    like = jax.ShapeDtypeStruct((1, TOK, D), BF16)
    return pl.pallas_call(
        kernel,
        out_shape=(like, like, like, like, jax.ShapeDtypeStruct((D, D), F32)),
        in_specs=[pl.BlockSpec(memory_space=pltpu.SMEM)] + [vmem] * 5,
        out_specs=(vmem,) * 5,
        scratch_shapes=[
            pltpu.VMEM((WIN, D), BF16), pltpu.VMEM((WIN, D), BF16),
            pltpu.VMEM((TOK, D), BF16), pltpu.VMEM((TOK, D), BF16), pltpu.VMEM((2 * TOK, WIN), F32),
            pltpu.VMEM((2, 2, TOK, D), BF16), pltpu.VMEM((2, 2, TOK, D), BF16), pltpu.VMEM((2, TOK, D), F32),
            pltpu.VMEM((PAIRS, 128, 256), BF16), pltpu.VMEM((PAIRS, 128, 256), BF16), pltpu.VMEM((PAIRS, 128, 256), F32),
            pltpu.VMEM((PAIRS, 128, 256), BF16), pltpu.VMEM((PAIRS, NX - 1, 32, 256), BF16), pltpu.VMEM((PAIRS, 128, 256), F32),
            pltpu.VMEM((PAIRS, 32, 256), BF16), pltpu.VMEM((NY - 1, 16, 256), BF16), pltpu.VMEM((16, 256), F32),
            pltpu.VMEM((NZ, 16, 256), BF16), pltpu.VMEM((NC, NX, NY, 16, 256), BF16),
            dma((PAIRS, 2, 2)), dma((PAIRS, 2, 2)), dma((PAIRS, 2, 2)), dma((PAIRS, 2, 2)),
            dma((PAIRS,)), dma((PAIRS,)), dma((PAIRS, NX - 1)), dma((PAIRS, NX - 1)),
            dma((PAIRS, 2)), dma((NY - 1,)), dma((NZ - 1,)), dma((NZ,)),
            dma((NY - 1,)), dma((NY,)), dma((NX - 1,)), dma((NX,)), dma, dma,
        ],
        compiler_params=pltpu.CompilerParams(
            collective_id=0, has_side_effects=True, vmem_limit_bytes=32 * 2**20
        ),
    )(table, query, key, value, out_weight, cotangent)


def solution(mesh):
    rows = P("dp", "ctx", None)
    return jax.shard_map(
        body,
        mesh=mesh,
        in_specs=(rows, rows, rows, P("ctx", None), P(), rows),
        out_specs=(rows, rows, rows, rows, P()),
        check_vma=False,
    )
```

time: 605 us -> 114 us (0.19)
  waiting for transfers between devices: 509 us -> 0 us
  Pallas kernels: 0 us -> 104 us
  starting transfers between devices: 32.3 us -> 0 us
  matrix products: 24.1 us -> 0 us
  between operations: 14.4 us -> 0.66 us
  local copies, waits for them, and re-layouts: 20.2 us -> 8.92 us
    psum x1 -> x0, waiting for transfers between devices: 465 us -> none  [body(): weight_total = lax.psum(weight_term, ('ctx', 'dp'))]
    pallas_call x0 -> x1, Pallas kernels: none -> 104 us  [body(): pl.pallas_call(kernel, out_shape=(like, like, like, like, jax.ShapeDtypeS...]
    ppermute x4 -> x0, waiting for transfers between devices: 43.2 us -> none  [the longest x1 16.2 us: with_halo(): before = lax.ppermute(last, axis, up)]
    ppermute x4 -> x0, starting transfers between devices: 32.2 us -> none  [the longest x1 25 us: with_halo(): after = lax.ppermute(initial, axis, down)]
    dot_general x11 -> x0, matrix products: 24.1 us -> none  [the longest x1 8.12 us: local_pass(): jnp.einsum('bhqk,bqhe->bkhe', dscore, query_blocks, preferred_element_typ...]
    reshape x9 -> x0, local copies, waits for them, and re-layouts: 7.69 us -> none  [the longest x1 1.93 us: local_pass(): value_terms = jnp.einsum('bhqk,bqhe->bkhe', rounded, grad_blocks, preferr...]
    unnamed x15 -> x17, local copies, waits for them, and re-layouts: 1.24 us -> 8.92 us
  transfers between devices with their start and end apart: 5 -> 0, of which waited for: 4 -> 0; matrix products, arithmetic and copies ran while one was open for 2% -> 0% of each run, Pallas kernels for 0% -> 0%
where the time goes in v1:
time: 114 us
  Pallas kernels  104 us (91%)
  local copies, waits for them, and re-layouts  8.92 us (8%)
    pallas_call x1, Pallas kernels, body(): pl.pallas_call(kernel, out_shape=(like, like, like, like, jax.ShapeDtypeS...  104 us
    unnamed x17, local copies, waits for them, and re-layouts  8.92 us

profile of v1, /device:TPU:1, one launch (start us, length us, event | category | flops | bytes accessed | tf_op | source)
XLA Modules:
  0.0 113.9 jit_solution(4015629849545248689)
XLA Ops:
  0.6 0.0 copy-start
  0.6 1.0 copy-done
  1.7 0.0 copy-start.1
  1.7 0.9 copy-done.1
  2.6 0.0 copy-start.2
  2.6 0.9 copy-done.2
  3.5 0.0 copy-start.3
  3.5 0.9 copy-done.3
  4.4 0.0 copy-start.4
  4.4 0.9 copy-done.4
  5.3 0.0 copy-start.5
  5.3 0.7 copy-done.5
  6.0 104.3 %shard_map.101 = (bf16[1,128,512]{2,1,0:T(8,128)(2,1)S(1)}, bf16[1,128,512]{2,1,0:T(8,128)(2,1)S(1)}, bf16[1,128,512]{2,1,0:T(8,128)(2,1)S(1)}, bf16[1,128,512]{2,1,0:T(8,128)(2,1)S(1)}, f32[512,512]{1,0:T(8,128)S(1)}) custom-call(s32[2,4]{1,0:T(2,128)S(1)} %copy-done.5, bf16[1,128,512]{2,1,0:T(8,128)(2,1)S(1)} %copy-done.1, ...), custom_call_target="tpu_custom_call" | custom-call | tf_op jit(solution)/shard_map/pallas_call | solution.py:280
  110.3 0.7 copy.16
  111.0 0.7 copy.17
  111.6 0.7 copy.18
  112.3 0.7 copy.19
  112.9 1.0 copy.20
Async XLA Ops:
  0.6 1.0 copy-start
  1.7 0.9 copy-start.1
  2.6 0.9 copy-start.2
  3.5 0.9 copy-start.3
  4.4 0.9 copy-start.4
  5.3 0.7 copy-start.5

commit v2 on v1

--- a/solution.py
+++ b/solution.py
@@ -46,12 +46,12 @@
 
 
 def kernel(
-    table, q, k, v, w, cot,
-    layer_out, grad_q, grad_k, grad_v, grad_w,
-    kwin, vwin, g, attn, bias,
+    table_in, q_in, k_in, v_in, w_in, cot_in,
+    layer_out, grad_q, grad_k, grad_v, gw,
+    table, q, w, cot, kwin, vwin, g, attn, bias,
     part_out, part_in, own,
-    c_out, c_in, c_own, x_out, x_in, x_own, y_out, y_in, y_own, zall, gw,
-    kv_s, kv_r, part_s, part_r, c_s, c_r, x_s, x_r, y_s, y_r, z_s, z_r,
+    c_out, c_in, c_own, x_out, x_in, x_own, y_out, y_in, y_own, zall,
+    relay, in_s, kv_s, kv_r, fwd_s, to_relay_s, relay_r, relay_s, part_s, part_r, c_s, c_r, x_s, x_r, y_s, y_r, z_s, z_r,
     gy_s, gy_r, gx_s, gx_r, gc_s, gc_r,
 ):
     ctx, dp, x, y, z, c = place()
@@ -63,13 +63,25 @@
     ys = [lax.rem(y + i, NY) for i in range(NY)]
     zs = [lax.rem(z + i, NZ) for i in range(NZ)]
 
+    first, second, third, last = x == 0, x == 1, x == 2, x == NX - 1
+    far = jnp.where(x < 2, lax.rem(ctx + n_ctx - 2, n_ctx), lax.rem(ctx + 2, n_ctx)), dp
+
     barrier = pltpu.get_barrier_semaphore()
-    peers = [before, after, other]
+    peers = [before, after, far]
+    peers += [at(x, y, i, c) for i in zs[1:]]
+    peers += [at(x, i, z, c) for i in ys[1:]]
     peers += [at(i, y, z, c) for i in xs[1:]]
-    peers += [at(x, i, z, c) for i in ys[1:]]
-    peers += [at(x, y, i, c) for i in zs[1:]]
+    peers += [other]
     for peer in peers:
         pl.semaphore_signal(barrier, 1, device_id=peer, device_id_type=MESH)
+    loads = []
+    for i, (src, dst) in enumerate((
+        (k_in.at[0], kwin.at[pl.ds(TOK, TOK)]), (v_in.at[0], vwin.at[pl.ds(TOK, TOK)]),
+        (cot_in.at[0], cot.at[0]), (w_in, w), (q_in.at[0], q.at[0]), (table_in, table),
+    )):
+        copy = pltpu.make_async_copy(src, dst, in_s.at[i])
+        copy.start()
+        loads.append(copy)
     pl.semaphore_wait(barrier, len(peers))
 
     def remote(src, dst, ssem, rsem, to):
@@ -80,21 +92,33 @@
     def lanes(p):
         return pl.ds(p * 128, 128)
 
-    halo = []
+    wins = (kwin, vwin)
+    starts = (0, 2 * TOK)
+
+    def halo(p, i, j):
+        return remote(
+            (k_in, v_in)[i].at[0, :, lanes(p)], wins[i].at[pl.ds(starts[j], TOK), lanes(p)],
+            kv_s.at[p, i, j], kv_r.at[p, i, j], (after, before)[j],
+        )
+
+    def handed_on(p, j):
+        rows = wins[1].at[pl.ds(starts[1 - j], TOK), lanes(p)]
+        return remote(rows, wins[1].at[pl.ds(starts[j], TOK), lanes(p)], fwd_s.at[p], kv_r.at[p, 1, j], far)
+
     for p in range(PAIRS):
-        row = []
-        for i, (src, win) in enumerate(((k, kwin), (v, vwin))):
-            for j, (to, start) in enumerate(((after, 0), (before, 2 * TOK))):
-                row.append(remote(
-                    src.at[0, :, lanes(p)], win.at[pl.ds(start, TOK), lanes(p)],
-                    kv_s.at[p, i, j], kv_r.at[p, i, j], to,
-                ))
-        for copy in row:
-            copy.start()
-        halo.append(row)
-
-    kwin[pl.ds(TOK, TOK), :] = k[0]
-    vwin[pl.ds(TOK, TOK), :] = v[0]
+        halo(p, 0, 0).start()
+        halo(p, 0, 1).start()
+
+        @pl.when(jnp.logical_not(last))
+        def _():
+            halo(p, 1, 0).start()
+
+        @pl.when(jnp.logical_not(first))
+        def _():
+            halo(p, 1, 1).start()
+
+    for copy in loads:
+        copy.wait()
     g[...] = nt(cot[0], w[...]).astype(BF16)
 
     block = lax.broadcasted_iota(jnp.int32, (BS, WIN), 1) // BS
@@ -123,9 +147,58 @@
         copy.start()
         pending.append(copy)
 
+    @pl.when(third)
+    def _():
+        for p in range(PAIRS):
+            halo(p, 1, 1).wait_recv()
+            handed_on(p, 0).start()
+
+    @pl.when(second)
+    def _():
+        for p in range(PAIRS):
+            halo(p, 1, 0).wait_recv()
+            handed_on(p, 1).start()
+
+    def part(p, i, j):
+        return remote(
+            part_out.at[i, j, :, lanes(p)], part_in.at[i, j, :, lanes(p)],
+            part_s.at[p, i, j], part_r.at[p, i, j], (before, after)[j],
+        )
+
+    def to_relay(p, j):
+        return remote(
+            part_out.at[1, j, :, lanes(p)], relay.at[:, lanes(p)],
+            to_relay_s.at[p], relay_r.at[p], (after, before)[j],
+        )
+
+    def from_relay(p, j):
+        return remote(
+            relay.at[:, lanes(p)], part_in.at[1, j, :, lanes(p)], relay_s.at[p], part_r.at[p, 1, j], far
+        )
+
+    def hand_on_part(p):
+        @pl.when(third)
+        def _():
+            to_relay(p, 1).wait_recv()
+            from_relay(p, 1).start()
+
+        @pl.when(second)
+        def _():
+            to_relay(p, 0).wait_recv()
+            from_relay(p, 0).start()
+
     def attention(p):
-        for copy in halo[p]:
-            copy.wait_recv()
+        halo(p, 0, 0).wait_recv()
+        halo(p, 0, 1).wait_recv()
+
+        @pl.when(jnp.logical_not(second))
+        def _():
+            halo(p, 1, 0).wait_recv()
+
+        @pl.when(jnp.logical_not(third))
+        def _():
+            halo(p, 1, 1).wait_recv()
+
         l = lanes(p)
         kw, vw = kwin[:, l], vwin[:, l]
         q2 = split(q[0, :, l] * jnp.asarray(0.125, BF16))
@@ -150,11 +223,25 @@
             part_out[i, 0, :, l] = d[:TOK].astype(BF16)
             part_out[i, 1, :, l] = d[2 * TOK:].astype(BF16)
             own[i, :, l] = d[TOK:2 * TOK]
-            for j, to in enumerate((before, after)):
-                send(remote(
-                    part_out.at[i, j, :, l], part_in.at[i, j, :, l],
-                    part_s.at[p, i, j], part_r.at[p, i, j], to,
-                ))
+        part(p, 0, 0).start()
+        part(p, 0, 1).start()
+
+        @pl.when(first)
+        def _():
+            to_relay(p, 0).start()
+
+        @pl.when(jnp.logical_not(first))
+        def _():
+            part(p, 1, 0).start()
+
+        @pl.when(last)
+        def _():
+            to_relay(p, 1).start()
+
+        @pl.when(jnp.logical_not(last))
+        def _():
+            part(p, 1, 1).start()
+
         grad_q[0, :, l] = (merged(nn(ds, kw)) * 0.125).astype(BF16)
 
     def core_step(p):
@@ -224,13 +311,17 @@
 
     attention(0)
     attention(1)
+    hand_on_part(0)
     core_step(0)
     attention(2)
+    hand_on_part(1)
     core_step(1)
     x_step(0)
     attention(3)
+    hand_on_part(2)
     core_step(2)
     x_step(1)
+    hand_on_part(3)
     core_step(3)
     x_step(2)
     x_step(3)
@@ -242,25 +333,37 @@
 
     for p in range(PAIRS):
         for i in range(2):
-            for j, to in enumerate((before, after)):
-                remote(
-                    part_out.at[i, j, :, lanes(p)], part_in.at[i, j, :, lanes(p)],
-                    part_s.at[p, i, j], part_r.at[p, i, j], to,
-                ).wait_recv()
+            for j in range(2):
+                part(p, i, j).wait_recv()
     for i, out in enumerate((grad_k, grad_v)):
         out[0] = (own[i] + part_in[i, 0].astype(F32) + part_in[i, 1].astype(F32)).astype(BF16)
 
     remote(gw.at[c], gw.at[1 - c], gc_s, gc_r, other).wait_recv()
-    scale = 1.0 / math.sqrt(TOK * NX * NY * NZ * NC)
-    for ci in range(NC):
-        for yi in range(NY):
-            for xi in range(NX):
-                row = (yi // 2) * 128 + xi * 32 + (yi % 2) * 16
-                grad_w[row:row + 16, ci * 256:ci * 256 + 256] = gw[ci, xi, yi].astype(F32) * scale
-
-    for row in halo:
-        for copy in row:
-            copy.wait_send()
+    for p in range(PAIRS):
+        for j in range(2):
+            halo(p, 0, j).wait_send()
+            part(p, 0, j).wait_send()
+
+        @pl.when(first)
+        def _():
+            halo(p, 1, 0).wait_send()
+            part(p, 1, 1).wait_send()
+            to_relay(p, 0).wait_send()
+
+        @pl.when(last)
+        def _():
+            halo(p, 1, 1).wait_send()
+            part(p, 1, 0).wait_send()
+            to_relay(p, 1).wait_send()
+
+        @pl.when(jnp.logical_or(second, third))
+        def _():
+            for j in range(2):
+                halo(p, 1, j).wait_send()
+                part(p, 1, j).wait_send()
+            handed_on(p, 0).wait_send()
+            from_relay(p, 0).wait_send()
+
     for copy in pending:
         copy.wait_send()
     for p in range(PAIRS):
@@ -273,32 +376,55 @@
                 ).wait_send()
 
 
+def finish(layer_out_in, grad_q_in, grad_k_in, grad_v_in, gw, layer_out, grad_q, grad_k, grad_v, grad_w):
+    layer_out[...] = layer_out_in[...]
+    grad_q[...] = grad_q_in[...]
+    grad_k[...] = grad_k_in[...]
+    grad_v[...] = grad_v_in[...]
+    scale = 1.0 / math.sqrt(TOK * NX * NY * NZ * NC)
+    for ci in range(NC):
+        for yi in range(NY):
+            for xi in range(NX):
+                row = (yi // 2) * 128 + xi * 32 + (yi % 2) * 16
+                grad_w[row:row + 16, ci * 256:ci * 256 + 256] = gw[ci, xi, yi].astype(F32) * scale
+
+
 def body(query, key, value, table, out_weight, cotangent):
     vmem = pl.BlockSpec(memory_space=pltpu.VMEM)
     dma = pltpu.SemaphoreType.DMA
     like = jax.ShapeDtypeStruct((1, TOK, D), BF16)
-    return pl.pallas_call(
+    shapes = (like, like, like, like)
+    anywhere = pl.BlockSpec(memory_space=pl.ANY)
+    raw = pl.pallas_call(
         kernel,
-        out_shape=(like, like, like, like, jax.ShapeDtypeStruct((D, D), F32)),
-        in_specs=[pl.BlockSpec(memory_space=pltpu.SMEM)] + [vmem] * 5,
+        out_shape=shapes + (jax.ShapeDtypeStruct((NC, NX, NY, 16, 256), BF16),),
+        in_specs=[anywhere] * 6,
         out_specs=(vmem,) * 5,
         scratch_shapes=[
+            pltpu.SMEM((2, 4), jnp.int32),
+            pltpu.VMEM((1, TOK, D), BF16), pltpu.VMEM((D, D), BF16), pltpu.VMEM((1, TOK, D), BF16),
             pltpu.VMEM((WIN, D), BF16), pltpu.VMEM((WIN, D), BF16),
             pltpu.VMEM((TOK, D), BF16), pltpu.VMEM((TOK, D), BF16), pltpu.VMEM((2 * TOK, WIN), F32),
             pltpu.VMEM((2, 2, TOK, D), BF16), pltpu.VMEM((2, 2, TOK, D), BF16), pltpu.VMEM((2, TOK, D), F32),
             pltpu.VMEM((PAIRS, 128, 256), BF16), pltpu.VMEM((PAIRS, 128, 256), BF16), pltpu.VMEM((PAIRS, 128, 256), F32),
             pltpu.VMEM((PAIRS, 128, 256), BF16), pltpu.VMEM((PAIRS, NX - 1, 32, 256), BF16), pltpu.VMEM((PAIRS, 128, 256), F32),
             pltpu.VMEM((PAIRS, 32, 256), BF16), pltpu.VMEM((NY - 1, 16, 256), BF16), pltpu.VMEM((16, 256), F32),
-            pltpu.VMEM((NZ, 16, 256), BF16), pltpu.VMEM((NC, NX, NY, 16, 256), BF16),
-            dma((PAIRS, 2, 2)), dma((PAIRS, 2, 2)), dma((PAIRS, 2, 2)), dma((PAIRS, 2, 2)),
+            pltpu.VMEM((NZ, 16, 256), BF16),
+            pltpu.VMEM((TOK, D), BF16), dma((6,)), dma((PAIRS, 2, 2)), dma((PAIRS, 2, 2)),
+            dma((PAIRS,)), dma((PAIRS,)), dma((PAIRS,)), dma((PAIRS,)),
+            dma((PAIRS, 2, 2)), dma((PAIRS, 2, 2)),
             dma((PAIRS,)), dma((PAIRS,)), dma((PAIRS, NX - 1)), dma((PAIRS, NX - 1)),
             dma((PAIRS, 2)), dma((NY - 1,)), dma((NZ - 1,)), dma((NZ,)),
             dma((NY - 1,)), dma((NY,)), dma((NX - 1,)), dma((NX,)), dma, dma,
         ],
-        compiler_params=pltpu.CompilerParams(
-            collective_id=0, has_side_effects=True, vmem_limit_bytes=32 * 2**20
-        ),
+        compiler_params=pltpu.CompilerParams(collective_id=0, has_side_effects=True),
     )(table, query, key, value, out_weight, cotangent)
+    return tuple(pl.pallas_call(
+        finish,
+        out_shape=shapes + (jax.ShapeDtypeStruct((D, D), F32),),
+        in_specs=[vmem] * 5,
+        out_specs=(vmem,) * 5,
+    )(*raw))
 
 
 def solution(mesh):

time: 114 us -> 91.1 us (0.80)
  Pallas kernels: 104 us -> 90.3 us
  local copies, waits for them, and re-layouts: 8.92 us -> 0 us
    pallas_call x1 -> x2, Pallas kernels: 104 us -> 90.3 us  [the longest x1 87.8 us: body(): pl.pallas_call(kernel, out_shape=shapes + (jax.ShapeDtypeStruct((NC, NX,...]
    unnamed x17 -> x0, local copies, waits for them, and re-layouts: 8.92 us -> none
where the time goes in v2:
time: 91.1 us; the launch traced here: 90.9 us
  Pallas kernels  90.3 us (99%)
    pallas_call x1, Pallas kernels, body(): pl.pallas_call(kernel, out_shape=shapes + (jax.ShapeDtypeStruct((NC, NX,...  87.8 us
    pallas_call x1, Pallas kernels, body(): pl.pallas_call(finish, out_shape=shapes + (jax.ShapeDtypeStruct((D, D), F...  2.46 us

profile of v2, /device:TPU:1, one launch (start us, length us, event | category | flops | bytes accessed | tf_op | source)
XLA Modules:
  0.0 90.9 jit_solution(5059426504054394391)
XLA Ops:
  0.6 87.8 %shard_map.101 = (bf16[1,128,512]{2,1,0:T(8,128)(2,1)}, bf16[1,128,512]{2,1,0:T(8,128)(2,1)}, bf16[1,128,512]{2,1,0:T(8,128)(2,1)}, bf16[1,128,512]{2,1,0:T(8,128)(2,1)}, bf16[2,4,8,16,256]{4,3,2,1,0:T(8,128)(2,1)}) custom-call(s32[2,4]{1,0:T(2,128)} %table_in.1, bf16[1,128,512]{2,1,0:T(8,128)(2,1)} %q_in.1, bf16[1,128,512]{2,1,0:T(8,128)(2,1)} %k_in.1, ...), custom_call_target="tpu_custom_call" | custom-call | tf_op jit(solution)/shard_map/pallas_call | solution.py:398
  88.5 2.5 %shard_map.102 = (bf16[1,128,512]{2,1,0:T(8,128)(2,1)}, bf16[1,128,512]{2,1,0:T(8,128)(2,1)}, bf16[1,128,512]{2,1,0:T(8,128)(2,1)}, bf16[1,128,512]{2,1,0:T(8,128)(2,1)}, f32[512,512]{1,0:T(8,128)}) custom-call(bf16[1,128,512]{2,1,0:T(8,128)(2,1)} %get-tuple-element.10.layer_out_in, bf16[1,128,512]{2,1,0:T(8,128)(2,1)} %get-tuple-element.11.grad_q_in, ...), custom_call_target="tpu_custom_call" | custom-call | tf_op jit(solution)/shard_map/pallas_call | solution.py:422

commit v3 on v2

--- a/solution.py
+++ b/solution.py
@@ -62,15 +62,18 @@
     xs = [lax.rem(x + i, NX) for i in range(NX)]
     ys = [lax.rem(y + i, NY) for i in range(NY)]
     zs = [lax.rem(z + i, NZ) for i in range(NZ)]
+    x_away = sorted(range(1, NX), key=lambda i: -min(i, NX - i))
+    y_away = sorted(range(1, NY), key=lambda i: -min(i, NY - i))
+    z_away = sorted(range(1, NZ), key=lambda i: -min(i, NZ - i))
 
     first, second, third, last = x == 0, x == 1, x == 2, x == NX - 1
     far = jnp.where(x < 2, lax.rem(ctx + n_ctx - 2, n_ctx), lax.rem(ctx + 2, n_ctx)), dp
 
     barrier = pltpu.get_barrier_semaphore()
     peers = [before, after, far]
-    peers += [at(x, y, i, c) for i in zs[1:]]
-    peers += [at(x, i, z, c) for i in ys[1:]]
-    peers += [at(i, y, z, c) for i in xs[1:]]
+    peers += [at(x, y, zs[i], c) for i in z_away]
+    peers += [at(x, ys[i], z, c) for i in y_away]
+    peers += [at(xs[i], y, z, c) for i in x_away]
     peers += [other]
     for peer in peers:
         pl.semaphore_signal(barrier, 1, device_id=peer, device_id_type=MESH)
@@ -223,6 +226,9 @@
             part_out[i, 0, :, l] = d[:TOK].astype(BF16)
             part_out[i, 1, :, l] = d[2 * TOK:].astype(BF16)
             own[i, :, l] = d[TOK:2 * TOK]
+        grad_q[0, :, l] = (merged(nn(ds, kw)) * 0.125).astype(BF16)
+
+    def send_parts(p):
         part(p, 0, 0).start()
         part(p, 0, 1).start()
 
@@ -241,15 +247,13 @@
         @pl.when(jnp.logical_not(last))
         def _():
             part(p, 1, 1).start()
-
-        grad_q[0, :, l] = (merged(nn(ds, kw)) * 0.125).astype(BF16)
 
     def core_step(p):
         remote(c_out.at[p], c_in.at[p], c_s.at[p], c_r.at[p], other).wait_recv()
         total = c_own[p] + c_in[p].astype(F32)
         x_own[p] = total
         x_out[p] = total.astype(BF16)
-        for i in range(1, NX):
+        for i in x_away:
             send(remote(
                 x_out.at[p, pl.ds(xs[i] * 32, 32)], x_in.at[p, i - 1],
                 x_s.at[p, i - 1], x_r.at[p, i - 1], at(xs[i], y, z, c),
@@ -279,57 +283,94 @@
                     y_s.at[p, half], y_r.at[slot], at(x, owner, z, c),
                 ).start()
 
-    def y_step():
-        total = y_own[...]
-        for i in range(NY - 1):
-            remote(y_out.at[0, pl.ds(0, 16)], y_in.at[i], y_s.at[0, 0], y_r.at[i], other).wait_recv()
-            total = total + y_in[i].astype(F32)
-        zall[z] = total.astype(BF16)
-        for i in range(1, NZ):
-            send(remote(zall.at[z], zall.at[z], z_s.at[i - 1], z_r.at[z], at(x, y, zs[i], c)))
-
-    def z_step():
-        for i in range(1, NZ):
-            remote(zall.at[z], zall.at[zs[i]], z_s.at[0], z_r.at[zs[i]], other).wait_recv()
-        total = zall[0].astype(F32)
-        for i in range(1, NZ):
-            total = total + zall[i].astype(F32)
-        gw[c, x, y] = total.astype(BF16)
-        for i in range(1, NY):
-            send(remote(gw.at[c, x, y], gw.at[c, x, y], gy_s.at[i - 1], gy_r.at[y], at(x, ys[i], z, c)))
-
-    def gather_x():
-        for i in range(1, NY):
-            remote(gw.at[c, x, y], gw.at[c, x, ys[i]], gy_s.at[0], gy_r.at[ys[i]], other).wait_recv()
-        for i in range(1, NX):
-            send(remote(gw.at[c, x], gw.at[c, x], gx_s.at[i - 1], gx_r.at[x], at(xs[i], y, z, c)))
-
-    def gather_core():
-        for i in range(1, NX):
-            remote(gw.at[c, x], gw.at[c, xs[i]], gx_s.at[0], gx_r.at[xs[i]], other).wait_recv()
-        send(remote(gw.at[c], gw.at[c], gc_s, gc_r, other))
+    def owns(p):
+        return jnp.logical_or(y == 2 * p, y == 2 * p + 1)
+
+    def to_z(i):
+        return remote(zall.at[z], zall.at[z], z_s.at[i - 1], z_r.at[z], at(x, y, zs[i], c))
+
+    def to_y(i):
+        return remote(gw.at[c, x, y], gw.at[c, x, y], gy_s.at[i - 1], gy_r.at[y], at(x, ys[i], z, c))
+
+    def y_step(p):
+        @pl.when(owns(p))
+        def _():
+            total = y_own[...]
+            for i in range(NY - 1):
+                remote(y_out.at[0, pl.ds(0, 16)], y_in.at[i], y_s.at[0, 0], y_r.at[i], other).wait_recv()
+                total = total + y_in[i].astype(F32)
+            zall[z] = total.astype(BF16)
+            for i in z_away:
+                to_z(i).start()
+
+    def z_step(p):
+        @pl.when(owns(p))
+        def _():
+            for i in range(1, NZ):
+                remote(zall.at[z], zall.at[zs[i]], z_s.at[0], z_r.at[zs[i]], other).wait_recv()
+            total = zall[0].astype(F32)
+            for i in range(1, NZ):
+                total = total + zall[i].astype(F32)
+            gw[c, x, y] = total.astype(BF16)
+            for i in y_away:
+                to_y(i).start()
+
+    def gather_x(p):
+        for yi in (2 * p, 2 * p + 1):
+            @pl.when(y != yi)
+            def _():
+                remote(gw.at[c, x, y], gw.at[c, x, yi], gy_s.at[0], gy_r.at[yi], other).wait_recv()
+
+            for i in x_away:
+                send(remote(
+                    gw.at[c, x, yi], gw.at[c, x, yi], gx_s.at[yi, i - 1], gx_r.at[yi, x], at(xs[i], y, z, c)
+                ))
+
+    def gather_core(p):
+        for yi in (2 * p, 2 * p + 1):
+            for i in range(1, NX):
+                remote(
+                    gw.at[c, x, yi], gw.at[c, xs[i], yi], gx_s.at[yi, 0], gx_r.at[yi, xs[i]], other
+                ).wait_recv()
+            send(remote(gw.at[c, :, yi], gw.at[c, :, yi], gc_s.at[yi], gc_r.at[yi], other))
 
     attention(0)
+    send_parts(0)
     attention(1)
+    send_parts(1)
+    attention(2)
+    send_parts(2)
+    attention(3)
+    send_parts(3)
+    core_step(0)
+    core_step(1)
+    core_step(2)
+    core_step(3)
     hand_on_part(0)
-    core_step(0)
-    attention(2)
     hand_on_part(1)
-    core_step(1)
     x_step(0)
-    attention(3)
-    hand_on_part(2)
-    core_step(2)
     x_step(1)
-    hand_on_part(3)
-    core_step(3)
     x_step(2)
     x_step(3)
-    y_step()
+    hand_on_part(2)
+    hand_on_part(3)
+    y_step(0)
+    y_step(1)
+    y_step(2)
+    y_step(3)
     layer_out[0] = nn(attn[...], w[...]).astype(BF16)
-    z_step()
-    gather_x()
-    gather_core()
+    z_step(0)
+    z_step(1)
+    gather_x(0)
+    z_step(2)
+    gather_x(1)
+    z_step(3)
+    gather_x(2)
+    gather_core(0)
+    gather_x(3)
+    gather_core(1)
+    gather_core(2)
+    gather_core(3)
 
     for p in range(PAIRS):
         for i in range(2):
@@ -338,7 +379,8 @@
     for i, out in enumerate((grad_k, grad_v)):
         out[0] = (own[i] + part_in[i, 0].astype(F32) + part_in[i, 1].astype(F32)).astype(BF16)
 
-    remote(gw.at[c], gw.at[1 - c], gc_s, gc_r, other).wait_recv()
+    for yi in range(NY):
+        remote(gw.at[c, :, yi], gw.at[1 - c, :, yi], gc_s.at[yi], gc_r.at[yi], other).wait_recv()
     for p in range(PAIRS):
         for j in range(2):
             halo(p, 0, j).wait_send()
@@ -366,6 +408,10 @@
 
     for copy in pending:
         copy.wait_send()
+    for i in z_away:
+        to_z(i).wait_send()
+    for i in y_away:
+        to_y(i).wait_send()
     for p in range(PAIRS):
         for half in range(2):
             @pl.when(y != 2 * p + half)
@@ -376,17 +422,25 @@
                 ).wait_send()
 
 
-def finish(layer_out_in, grad_q_in, grad_k_in, grad_v_in, gw, layer_out, grad_q, grad_k, grad_v, grad_w):
-    layer_out[...] = layer_out_in[...]
-    grad_q[...] = grad_q_in[...]
-    grad_k[...] = grad_k_in[...]
-    grad_v[...] = grad_v_in[...]
+def finish(layer_out_in, grad_q_in, grad_k_in, grad_v_in, gw, layer_out, grad_q, grad_k, grad_v, grad_w, total, sems):
+    copies = []
+    for src, dst in (
+        (layer_out_in, layer_out), (grad_q_in, grad_q), (grad_k_in, grad_k), (grad_v_in, grad_v),
+    ):
+        copies.append(pltpu.make_async_copy(src, dst, sems.at[len(copies)]))
+        copies[-1].start()
     scale = 1.0 / math.sqrt(TOK * NX * NY * NZ * NC)
-    for ci in range(NC):
-        for yi in range(NY):
+    for yi in range(NY):
+        for ci in range(NC):
             for xi in range(NX):
                 row = (yi // 2) * 128 + xi * 32 + (yi % 2) * 16
-                grad_w[row:row + 16, ci * 256:ci * 256 + 256] = gw[ci, xi, yi].astype(F32) * scale
+                total[row:row + 16, ci * 256:ci * 256 + 256] = gw[ci, xi, yi].astype(F32) * scale
+        if yi % 2:
+            rows = pl.ds(yi // 2 * 128, 128)
+            copies.append(pltpu.make_async_copy(total.at[rows], grad_w.at[rows], sems.at[len(copies)]))
+            copies[-1].start()
+    for copy in copies:
+        copy.wait()
 
 
 def body(query, key, value, table, out_weight, cotangent):
@@ -415,7 +469,7 @@
             dma((PAIRS, 2, 2)), dma((PAIRS, 2, 2)),
             dma((PAIRS,)), dma((PAIRS,)), dma((PAIRS, NX - 1)), dma((PAIRS, NX - 1)),
             dma((PAIRS, 2)), dma((NY - 1,)), dma((NZ - 1,)), dma((NZ,)),
-            dma((NY - 1,)), dma((NY,)), dma((NX - 1,)), dma((NX,)), dma, dma,
+            dma((NY - 1,)), dma((NY,)), dma((NY, NX - 1)), dma((NY, NX)), dma((NY,)), dma((NY,)),
         ],
         compiler_params=pltpu.CompilerParams(collective_id=0, has_side_effects=True),
     )(table, query, key, value, out_weight, cotangent)
@@ -423,7 +477,8 @@
         finish,
         out_shape=shapes + (jax.ShapeDtypeStruct((D, D), F32),),
         in_specs=[vmem] * 5,
-        out_specs=(vmem,) * 5,
+        out_specs=(anywhere,) * 5,
+        scratch_shapes=[pltpu.VMEM((D, D), F32), dma((8,))],
     )(*raw))
 
 

time: 91.1 us -> 89.7 us (0.985)
  Pallas kernels: 90.3 us -> 88.9 us
    pallas_call x1, Pallas kernels: 87.8 us -> 86.4 us  [body(): pl.pallas_call(kernel, out_shape=shapes + (jax.ShapeDtypeStruct((NC, NX,...]
where the time goes in v3:
time: 89.7 us; the launch traced here: 89.5 us
  Pallas kernels  88.9 us (99%)
    pallas_call x1, Pallas kernels, body(): pl.pallas_call(kernel, out_shape=shapes + (jax.ShapeDtypeStruct((NC, NX,...  86.4 us
    pallas_call x1, Pallas kernels, body(): pl.pallas_call(finish, out_shape=shapes + (jax.ShapeDtypeStruct((D, D), F...  2.51 us

profile of v3, /device:TPU:1, one launch (start us, length us, event | category | flops | bytes accessed | tf_op | source)
XLA Modules:
  0.0 89.5 jit_solution(14517779289882711402)
XLA Ops:
  0.6 86.4 %shard_map.101 = (bf16[1,128,512]{2,1,0:T(8,128)(2,1)}, bf16[1,128,512]{2,1,0:T(8,128)(2,1)}, bf16[1,128,512]{2,1,0:T(8,128)(2,1)}, bf16[1,128,512]{2,1,0:T(8,128)(2,1)}, bf16[2,4,8,16,256]{4,3,2,1,0:T(8,128)(2,1)}) custom-call(s32[2,4]{1,0:T(2,128)} %table_in.1, bf16[1,128,512]{2,1,0:T(8,128)(2,1)} %q_in.1, bf16[1,128,512]{2,1,0:T(8,128)(2,1)} %k_in.1, ...), custom_call_target="tpu_custom_call" | custom-call | tf_op jit(solution)/shard_map/pallas_call | solution.py:452
  87.0 2.5 %shard_map.102 = (bf16[1,128,512]{2,1,0:T(8,128)(2,1)}, bf16[1,128,512]{2,1,0:T(8,128)(2,1)}, bf16[1,128,512]{2,1,0:T(8,128)(2,1)}, bf16[1,128,512]{2,1,0:T(8,128)(2,1)}, f32[512,512]{1,0:T(8,128)}) custom-call(bf16[1,128,512]{2,1,0:T(8,128)(2,1)} %get-tuple-element.10.layer_out_in, bf16[1,128,512]{2,1,0:T(8,128)(2,1)} %get-tuple-element.11.grad_q_in, ...), custom_call_target="tpu_custom_call" | custom-call | tf_op jit(solution)/shard_map/pallas_call | solution.py:476
